TPU v7x, 32 devices: a whole 2x2x4 slice. The times are simulated.
32 devices in a mesh: slab: 2 (over y), tm: 4 (over z), chan: 4 (over x, core).
Axes of the slice: x: 2, y: 2, z: 4, core: 2. Of those that a mesh axis runs over, the one named last changes fastest.
Arguments:
- record: bfloat16 [128, 4096], P('chan', ('slab', 'tm')), parts along dimension 1, may hold values from -6 to 6
- quality: int32 [128], P('chan'), may hold values 0 or 1
- fir_taps: float32 [129], replicated, may hold values from -0.5 to 0.5
- source_channels: int32 [128], replicated, may hold values from 0 to 127, as said below
Outputs:
- correlations: float32 [256, 128, 512], P(('slab', 'tm'), 'chan'), parts along dimension 0
There are 2 independent parts, one for each index of `slab`. A program takes and returns all parts, laid end to end along the dimension named above; an argument that names none is the same for every part. Nothing has to cross between parts.
Inputs may be any that keep to these rules, and one draw needn't show every extreme that they name: `source_channels`: distinct channel numbers.
All inputs are finite; a program needn't handle non-finite values. No bound on the sum of `quality` on one device may be relied on, other than what follows from the above.
Results may differ from a plain program's by a relative error of at most 0.0055.
Values may be sent and summed in bfloat16 or wider, within the bound.
A program may use at most 64 MiB of HBM per device.

v0:
```python
import functools
import math

import jax
import jax.numpy as jnp
from jax import lax
from jax.experimental import pallas as pl
from jax.experimental.pallas import tpu as pltpu
from jax.sharding import PartitionSpec as P

HALF = 256
LAGS = 2 * HALF
BLK = 128
PAD = 256
MESH = pl.DeviceIdType.MESH
NT = (((1,), (1,)), ((), ()))


def gather_kernel(n_tm, n_chan, rec_ref, keep_ref, out_ref, s_tm, r_tm, s_x, r_x, s_c, r_c):
    me_t = lax.axis_index("tm")
    me_c = lax.axis_index("chan")
    n_x = n_chan // 2
    core = lax.rem(me_c, 2)
    me_x = me_c // 2
    sibling = me_c + 1 - 2 * core

    def tm_peer(d):
        return {"tm": lax.rem(me_t + d, n_tm)}

    def x_peer(e):
        return {"chan": 2 * lax.rem(me_x + e, n_x) + core}

    barrier = pltpu.get_barrier_semaphore()
    peers = [tm_peer(d) for d in range(1, n_tm)] + [x_peer(e) for e in range(1, n_x)]
    peers.append({"chan": sibling})
    for peer in peers:
        pl.semaphore_signal(barrier, inc=1, device_id=peer, device_id_type=MESH)

    rows = rec_ref.shape[0]
    keep = jnp.broadcast_to(keep_ref[...].astype(jnp.float32), (rows, rows))
    first = lax.broadcasted_iota(jnp.int32, (rows, rows), 0)
    second = lax.broadcasted_iota(jnp.int32, (rows, rows), 1)
    diagonal = jnp.where(first == second, keep, 0.0).astype(jnp.bfloat16)
    out_ref[me_c, me_t] = jnp.dot(
        diagonal, rec_ref[...], preferred_element_type=jnp.float32
    ).astype(jnp.bfloat16)
    pl.semaphore_wait(barrier, len(peers))

    def slot(e, d):
        return out_ref.at[2 * lax.rem(me_x + n_x - e, n_x) + core, lax.rem(me_t + n_tm - d, n_tm)]

    def other_slot(e, d):
        return out_ref.at[
            2 * lax.rem(me_x + n_x - e, n_x) + 1 - core, lax.rem(me_t + n_tm - d, n_tm)
        ]

    def copy(ref, send, recv, peer):
        return pltpu.make_async_remote_copy(
            src_ref=ref, dst_ref=ref, send_sem=send, recv_sem=recv, device_id=peer,
            device_id_type=MESH,
        )

    sent = []

    def start(op):
        op.start()
        sent.append(op)

    def to_x(d):
        for e in range(1, n_x):
            start(copy(slot(0, d), s_x.at[e, d], r_x.at[e, d], x_peer(e)))

    def to_core(e, d):
        start(copy(slot(e, d), s_c.at[e, d], r_c.at[e, d], {"chan": sibling}))

    for d in range(n_tm - 1, 0, -1):
        start(copy(slot(0, 0), s_tm.at[d], r_tm.at[d], tm_peer(d)))
    to_x(0)
    to_core(0, 0)

    def from_x(d):
        for e in range(1, n_x):
            copy(slot(e, d), s_x.at[e, d], r_x.at[e, d], x_peer(e)).wait_recv()
            to_core(e, d)

    for d in range(1, n_tm):
        copy(slot(0, d), s_tm.at[d], r_tm.at[d], tm_peer(d)).wait_recv()
        to_x(d)
        to_core(0, d)
        from_x(d - 1)
    from_x(n_tm - 1)
    for e in range(n_x):
        for d in range(n_tm):
            copy(other_slot(e, d), s_c.at[e, d], r_c.at[e, d], {"chan": sibling}).wait_recv()
    for op in sent:
        op.wait_send()


def three_parts(value):
    high = value.astype(jnp.bfloat16)
    rest = value - high.astype(jnp.float32)
    middle = rest.astype(jnp.bfloat16)
    low = (rest - middle.astype(jnp.float32)).astype(jnp.bfloat16)
    return high, middle, low


def correlate_kernel(
    n_src, all_ref, taps_ref, src_ref, out_ref, taps_row, raw, rev, lhs, rhs_a, rhs_b
):
    n_chan, n_tm, rows, t_dev = all_ref.shape
    total = n_tm * t_dev
    n_ch = n_chan * rows
    panel_rows = src_ref.shape[1]
    padded_src = raw.shape[0] - rows
    blocks = total // BLK + 4
    wide = 2 * BLK
    window = 4 * BLK
    me_t = lax.axis_index("tm")
    me_c = lax.axis_index("chan")
    scale = 1.0 / math.sqrt(total)

    n_taps = taps_ref.shape[1]
    taps_row[...] = jnp.zeros_like(taps_row)
    taps_row[0:1, 0:n_taps] = taps_ref[...]
    spread = jnp.broadcast_to(taps_row[0:1, :], (wide, window))
    forward = pltpu.roll(spread, 64, 1, stride=1, stride_axis=0)
    shifted = pltpu.roll(spread, 65, 1, stride=1, stride_axis=0)
    flip = (
        lax.broadcasted_iota(jnp.int32, (wide, wide), 0)
        + lax.broadcasted_iota(jnp.int32, (wide, wide), 1)
        == wide - 1
    ).astype(jnp.float32).astype(jnp.bfloat16)
    forward_parts = three_parts(forward)
    backward_parts = [
        jnp.dot(flip, part, preferred_element_type=jnp.float32).astype(jnp.bfloat16)
        for part in three_parts(shifted)
    ]

    which = (
        lax.broadcasted_iota(jnp.int32, (n_ch, panel_rows), 0)
        == jnp.broadcast_to(src_ref[...], (n_ch, panel_rows))
    ).astype(jnp.float32).astype(jnp.bfloat16)
    mine = (
        lax.broadcasted_iota(jnp.int32, (padded_src, panel_rows), 0) + me_t * n_src
        == lax.broadcasted_iota(jnp.int32, (padded_src, panel_rows), 1)
    ).astype(jnp.float32).astype(jnp.bfloat16)
    selector = lax.dot_general(
        mine, which, NT, preferred_element_type=jnp.float32
    ).astype(jnp.bfloat16)

    raw[:, 0:PAD] = jnp.zeros((rows + padded_src, PAD), jnp.bfloat16)
    raw[:, PAD + total :] = jnp.zeros((rows + padded_src, PAD), jnp.bfloat16)
    for t in range(n_tm):
        at = slice(PAD + t * t_dev, PAD + (t + 1) * t_dev)
        raw[0:rows, at] = all_ref[me_c, t]
        raw[rows:, at] = jnp.dot(
            selector, all_ref[:, t].reshape(n_ch, t_dev), preferred_element_type=jnp.float32
        ).astype(jnp.bfloat16)

    def filtered(windows, parts):
        return sum(
            lax.dot_general(windows, part, NT, preferred_element_type=jnp.float32)
            for part in parts
        )

    lhs[...] = jnp.zeros_like(lhs)
    n_wide = total // wide
    group = 8
    for q0 in range(0, n_wide, group):
        windows = jnp.concatenate(
            [
                raw[0:rows, PAD + wide * q - BLK : PAD + wide * q - BLK + window]
                for q in range(q0, q0 + group)
            ],
            axis=0,
        )
        values = filtered(windows, forward_parts).astype(jnp.bfloat16)
        for i in range(group):
            for j in range(4):
                begin = BLK * (3 - j) + wide * (q0 + i)
                lhs[j * rows : (j + 1) * rows, begin : begin + wide] = values[
                    i * rows : (i + 1) * rows
                ]

    rev[:, 0:wide] = jnp.zeros((padded_src, wide), jnp.float32)
    end = wide * (n_wide + 2)
    rev[:, end:] = jnp.zeros((padded_src, rev.shape[1] - end), jnp.float32)
    for q0 in range(1, n_wide + 2, group):
        qs = range(q0, min(q0 + group, n_wide + 2))
        windows = jnp.concatenate(
            [
                raw[rows:, PAD + total - wide * q : PAD + total - wide * q + window]
                for q in qs
            ],
            axis=0,
        )
        values = filtered(windows, backward_parts).astype(jnp.bfloat16).astype(jnp.float32)
        for i, q in enumerate(qs):
            place = lax.broadcasted_iota(jnp.int32, (padded_src, wide), 1) + wide * q
            inside = (place >= 3 * BLK + 1) & (place <= total + 3 * BLK)
            rev[:, wide * q : wide * (q + 1)] = jnp.where(
                inside, values[i * padded_src : (i + 1) * padded_src], 0.0
            )

    width = BLK * (blocks + 1)

    def build(ref, pair):
        for h in range(2):
            row = rev[pl.ds(2 * pair + h, 1), 0:width]
            spread = jnp.broadcast_to(row, (16, width))
            steps = pltpu.roll(spread, 0, 1, stride=1, stride_axis=0)
            for k in range(8):
                moved = steps if k == 0 else pltpu.roll(steps, 16 * k, 1)
                moved = moved.astype(jnp.bfloat16)
                for m in range(blocks):
                    base = BLK * (blocks - m)
                    ref[BLK * m + 16 * k : BLK * m + 16 * (k + 1), BLK * h : BLK * (h + 1)] = (
                        moved[:, base : base + BLK]
                    )

    def multiply(ref, pair):
        result = jnp.dot(lhs[...], ref[...], preferred_element_type=jnp.float32) * scale
        for h in range(2):
            for j in range(4):
                out_ref[2 * pair + h, :, BLK * j : BLK * (j + 1)] = result[
                    j * rows : (j + 1) * rows, BLK * h : BLK * (h + 1)
                ]

    pairs = n_src // 2
    build(rhs_a, 0)

    def step(i, carry):
        multiply(rhs_a, 2 * i)
        build(rhs_b, 2 * i + 1)
        multiply(rhs_b, 2 * i + 1)
        build(rhs_a, jnp.minimum(2 * i + 2, pairs - 1))
        return carry

    lax.fori_loop(0, pairs // 2, step, 0)


def local(record, quality, fir_taps, source_channels):
    rows, t_dev = record.shape
    n_tm = lax.axis_size("tm")
    n_chan = lax.axis_size("chan")
    panel_rows = source_channels.shape[0]
    n_src = panel_rows // n_tm
    total = t_dev * n_tm
    blocks = total // BLK + 4
    vmem = pl.BlockSpec(memory_space=pltpu.VMEM)
    dma = pltpu.SemaphoreType.DMA
    everything = pl.pallas_call(
        functools.partial(gather_kernel, n_tm, n_chan),
        out_shape=jax.ShapeDtypeStruct((n_chan, n_tm, rows, t_dev), jnp.bfloat16),
        in_specs=[vmem] * 2,
        out_specs=vmem,
        scratch_shapes=[
            dma((n_tm,)),
            dma((n_tm,)),
            dma((n_chan // 2, n_tm)),
            dma((n_chan // 2, n_tm)),
            dma((n_chan // 2, n_tm)),
            dma((n_chan // 2, n_tm)),
        ],
        compiler_params=pltpu.CompilerParams(
            collective_id=0, has_side_effects=True, vmem_limit_bytes=32 * 2**20
        ),
        name="gather_records",
    )(record, quality.reshape(1, rows))
    padded_src = -(-n_src // 16) * 16
    return pl.pallas_call(
        functools.partial(correlate_kernel, n_src),
        out_shape=jax.ShapeDtypeStruct((n_src, rows, LAGS), jnp.float32),
        in_specs=[vmem] * 3,
        out_specs=vmem,
        scratch_shapes=[
            pltpu.VMEM((8, 4 * BLK), jnp.float32),
            pltpu.VMEM((rows + padded_src, total + 2 * PAD), jnp.bfloat16),
            pltpu.VMEM((padded_src, BLK * (blocks + 2)), jnp.float32),
            pltpu.VMEM((4 * rows, BLK * blocks), jnp.bfloat16),
            pltpu.VMEM((BLK * blocks, 2 * BLK), jnp.bfloat16),
            pltpu.VMEM((BLK * blocks, 2 * BLK), jnp.bfloat16),
        ],
        compiler_params=pltpu.CompilerParams(vmem_limit_bytes=56 * 2**20),
        name="correlate_all",
    )(everything, fir_taps.reshape(1, -1), source_channels.reshape(1, -1))


def solution(mesh):
    placed = (P("chan", ("slab", "tm")), P("chan"), P(), P())
    return jax.shard_map(
        local,
        mesh=mesh,
        in_specs=placed,
        out_specs=P(("slab", "tm"), "chan", None),
        check_vma=False,
    )
```

profile of v0, /device:TPU:1, one launch (start us, length us, event | category | flops | bytes accessed | tf_op | source)
XLA Modules:
  0.0 31.4 jit_solution(15173174668021284330)
XLA Ops:
  0.0 0.0 copy-start.1
  0.0 0.8 %copy-done.1 = bf16[32,512]{1,0:T(8,128)(2,1)S(1)} copy-done((bf16[32,512]{1,0:T(8,128)(2,1)S(1)}, bf16[32,512]{1,0:T(8,128)(2,1)}, u32[]{:S(2)}) %copy-start.1) | copy-done | bytes 32792
  0.8 0.0 copy-start.2
  0.8 0.7 %copy-done.2 = s32[32]{0:T(128)S(1)} copy-done((s32[32]{0:T(128)S(1)}, s32[32]{0:T(128)}, u32[]{:S(2)}) %copy-start.2) | copy-done | bytes 152
  1.4 16.1 %gather_records.1.all_ref = bf16[4,4,32,512]{3,2,1,0:T(8,128)(2,1)S(1)} custom-call(bf16[32,512]{1,0:T(8,128)(2,1)S(1)} %copy-done.1, s32[1,32]{1,0:T(1,128)S(1)} %bitcast.3), custom_call_target="tpu_custom_call" | custom-call | tf_op jit(solution)/shard_map/gather_records/pallas_call | solution.py:252
  17.5 0.0 copy-start
  17.5 0.8 %copy-done = bf16[4,4,32,512]{3,2,1,0:T(8,128)(2,1)} copy-done((bf16[4,4,32,512]{3,2,1,0:T(8,128)(2,1)}, bf16[4,4,32,512]{3,2,1,0:T(8,128)(2,1)S(1)}, u32[]{:S(2)}) %copy-start) | copy-done | bytes 524312
  18.3 13.1 %correlate_all.1 = f32[32,32,512]{2,1,0:T(8,128)} custom-call(bf16[4,4,32,512]{3,2,1,0:T(8,128)(2,1)} %copy-done, f32[1,129]{1,0:T(1,128)} %bitcast.4, s32[1,128]{1,0:T(1,128)} %bitcast.5), custom_call_target="tpu_custom_call" | custom-call | tf_op jit(solution)/shard_map/correlate_all/pallas_call | solution.py:271
Async XLA Ops:
  0.0 0.8 %copy-start.1 = (bf16[32,512]{1,0:T(8,128)(2,1)S(1)}, bf16[32,512]{1,0:T(8,128)(2,1)}, u32[]{:S(2)}) copy-start(bf16[32,512]{1,0:T(8,128)(2,1)} %rec_ref.1) | copy-start | bytes 98308
  0.8 0.7 %copy-start.2 = (s32[32]{0:T(128)S(1)}, s32[32]{0:T(128)}, u32[]{:S(2)}) copy-start(s32[32]{0:T(128)} %param.5) | copy-start | bytes 388
  17.5 0.8 %copy-start = (bf16[4,4,32,512]{3,2,1,0:T(8,128)(2,1)}, bf16[4,4,32,512]{3,2,1,0:T(8,128)(2,1)S(1)}, u32[]{:S(2)}) copy-start(bf16[4,4,32,512]{3,2,1,0:T(8,128)(2,1)S(1)} %gather_records.1.all_ref) | copy-start | bytes 1572868
where the time goes:
time: 31.7 us; the launch traced here: 31.4 us
  Pallas kernels  29.2 us (92%)
  local copies, waits for them, and re-layouts  2.2 us (7%)
    pallas_call x1, Pallas kernels, local(): pl.pallas_call(functools.partial(gather_kernel, n_tm, n_chan), out_shape=...  16.1 us
    pallas_call x1, Pallas kernels, local(): pl.pallas_call(functools.partial(correlate_kernel, n_src), out_shape=jax....  13.1 us
    unnamed x6, local copies, waits for them, and re-layouts  2.2 us

commit v1 on v0

--- a/solution.py
+++ b/solution.py
@@ -16,7 +16,23 @@
 NT = (((1,), (1,)), ((), ()))
 
 
-def gather_kernel(n_tm, n_chan, rec_ref, keep_ref, out_ref, s_tm, r_tm, s_x, r_x, s_c, r_c):
+def three_parts(value):
+    high = value.astype(jnp.bfloat16)
+    rest = value - high.astype(jnp.float32)
+    middle = rest.astype(jnp.bfloat16)
+    low = (rest - middle.astype(jnp.float32)).astype(jnp.bfloat16)
+    return high, middle, low
+
+
+def prepare_kernel(
+    n_src, n_tm, n_chan, rec_hbm, keep_hbm, taps_hbm, src_hbm, lhs, rev,
+    out_ref, rec_ref, keep_ref, taps_ref, src_ref, taps_row, raw, forward_ref, backward_ref,
+    l_sem, s_tm, r_tm, s_x, r_x, s_c, r_c,
+):
+    pairs = ((rec_hbm, rec_ref), (keep_hbm, keep_ref), (taps_hbm, taps_ref), (src_hbm, src_ref))
+    loads = [pltpu.make_async_copy(a, b, l_sem.at[i]) for i, (a, b) in enumerate(pairs)]
+    for load in loads:
+        load.start()
     me_t = lax.axis_index("tm")
     me_c = lax.axis_index("chan")
     n_x = n_chan // 2
@@ -36,7 +52,15 @@
     for peer in peers:
         pl.semaphore_signal(barrier, inc=1, device_id=peer, device_id_type=MESH)
 
-    rows = rec_ref.shape[0]
+    rows, t_dev = rec_ref.shape
+    total = n_tm * t_dev
+    n_ch = n_chan * rows
+    panel_rows = src_ref.shape[1]
+    padded_src = raw.shape[0] - rows
+    wide = 2 * BLK
+    window = 4 * BLK
+    loads[0].wait()
+    loads[1].wait()
     keep = jnp.broadcast_to(keep_ref[...].astype(jnp.float32), (rows, rows))
     first = lax.broadcasted_iota(jnp.int32, (rows, rows), 0)
     second = lax.broadcasted_iota(jnp.int32, (rows, rows), 1)
@@ -78,47 +102,8 @@
     to_x(0)
     to_core(0, 0)
 
-    def from_x(d):
-        for e in range(1, n_x):
-            copy(slot(e, d), s_x.at[e, d], r_x.at[e, d], x_peer(e)).wait_recv()
-            to_core(e, d)
-
-    for d in range(1, n_tm):
-        copy(slot(0, d), s_tm.at[d], r_tm.at[d], tm_peer(d)).wait_recv()
-        to_x(d)
-        to_core(0, d)
-        from_x(d - 1)
-    from_x(n_tm - 1)
-    for e in range(n_x):
-        for d in range(n_tm):
-            copy(other_slot(e, d), s_c.at[e, d], r_c.at[e, d], {"chan": sibling}).wait_recv()
-    for op in sent:
-        op.wait_send()
-
-
-def three_parts(value):
-    high = value.astype(jnp.bfloat16)
-    rest = value - high.astype(jnp.float32)
-    middle = rest.astype(jnp.bfloat16)
-    low = (rest - middle.astype(jnp.float32)).astype(jnp.bfloat16)
-    return high, middle, low
-
-
-def correlate_kernel(
-    n_src, all_ref, taps_ref, src_ref, out_ref, taps_row, raw, rev, lhs, rhs_a, rhs_b
-):
-    n_chan, n_tm, rows, t_dev = all_ref.shape
-    total = n_tm * t_dev
-    n_ch = n_chan * rows
-    panel_rows = src_ref.shape[1]
-    padded_src = raw.shape[0] - rows
-    blocks = total // BLK + 4
-    wide = 2 * BLK
-    window = 4 * BLK
-    me_t = lax.axis_index("tm")
-    me_c = lax.axis_index("chan")
-    scale = 1.0 / math.sqrt(total)
-
+    loads[2].wait()
+    loads[3].wait()
     n_taps = taps_ref.shape[1]
     taps_row[...] = jnp.zeros_like(taps_row)
     taps_row[0:1, 0:n_taps] = taps_ref[...]
@@ -130,11 +115,12 @@
         + lax.broadcasted_iota(jnp.int32, (wide, wide), 1)
         == wide - 1
     ).astype(jnp.float32).astype(jnp.bfloat16)
-    forward_parts = three_parts(forward)
-    backward_parts = [
-        jnp.dot(flip, part, preferred_element_type=jnp.float32).astype(jnp.bfloat16)
-        for part in three_parts(shifted)
-    ]
+    for i, part in enumerate(three_parts(forward)):
+        forward_ref[i] = part
+    for i, part in enumerate(three_parts(shifted)):
+        backward_ref[i] = jnp.dot(flip, part, preferred_element_type=jnp.float32).astype(
+            jnp.bfloat16
+        )
 
     which = (
         lax.broadcasted_iota(jnp.int32, (n_ch, panel_rows), 0)
@@ -150,20 +136,26 @@
 
     raw[:, 0:PAD] = jnp.zeros((rows + padded_src, PAD), jnp.bfloat16)
     raw[:, PAD + total :] = jnp.zeros((rows + padded_src, PAD), jnp.bfloat16)
-    for t in range(n_tm):
-        at = slice(PAD + t * t_dev, PAD + (t + 1) * t_dev)
-        raw[0:rows, at] = all_ref[me_c, t]
-        raw[rows:, at] = jnp.dot(
-            selector, all_ref[:, t].reshape(n_ch, t_dev), preferred_element_type=jnp.float32
-        ).astype(jnp.bfloat16)
+    lhs[...] = jnp.zeros_like(lhs)
 
     def filtered(windows, parts):
         return sum(
-            lax.dot_general(windows, part, NT, preferred_element_type=jnp.float32)
-            for part in parts
-        )
-
-    lhs[...] = jnp.zeros_like(lhs)
+            lax.dot_general(windows, parts[i], NT, preferred_element_type=jnp.float32)
+            for i in range(3)
+        )
+
+    def from_x(d):
+        for e in range(1, n_x):
+            copy(slot(e, d), s_x.at[e, d], r_x.at[e, d], x_peer(e)).wait_recv()
+            to_core(e, d)
+
+    for d in range(1, n_tm):
+        copy(slot(0, d), s_tm.at[d], r_tm.at[d], tm_peer(d)).wait_recv()
+        to_x(d)
+        to_core(0, d)
+        from_x(d - 1)
+    for t in range(n_tm):
+        raw[0:rows, PAD + t * t_dev : PAD + (t + 1) * t_dev] = out_ref[me_c, t]
     n_wide = total // wide
     group = 8
     for q0 in range(0, n_wide, group):
@@ -174,7 +166,7 @@
             ],
             axis=0,
         )
-        values = filtered(windows, forward_parts).astype(jnp.bfloat16)
+        values = filtered(windows, forward_ref).astype(jnp.bfloat16)
         for i in range(group):
             for j in range(4):
                 begin = BLK * (3 - j) + wide * (q0 + i)
@@ -182,6 +174,14 @@
                     i * rows : (i + 1) * rows
                 ]
 
+    from_x(n_tm - 1)
+    for e in range(n_x):
+        for d in range(n_tm):
+            copy(other_slot(e, d), s_c.at[e, d], r_c.at[e, d], {"chan": sibling}).wait_recv()
+    for t in range(n_tm):
+        raw[rows:, PAD + t * t_dev : PAD + (t + 1) * t_dev] = jnp.dot(
+            selector, out_ref[:, t].reshape(n_ch, t_dev), preferred_element_type=jnp.float32
+        ).astype(jnp.bfloat16)
     rev[:, 0:wide] = jnp.zeros((padded_src, wide), jnp.float32)
     end = wide * (n_wide + 2)
     rev[:, end:] = jnp.zeros((padded_src, rev.shape[1] - end), jnp.float32)
@@ -194,7 +194,7 @@
             ],
             axis=0,
         )
-        values = filtered(windows, backward_parts).astype(jnp.bfloat16).astype(jnp.float32)
+        values = filtered(windows, backward_ref).astype(jnp.bfloat16).astype(jnp.float32)
         for i, q in enumerate(qs):
             place = lax.broadcasted_iota(jnp.int32, (padded_src, wide), 1) + wide * q
             inside = (place >= 3 * BLK + 1) & (place <= total + 3 * BLK)
@@ -202,6 +202,14 @@
                 inside, values[i * padded_src : (i + 1) * padded_src], 0.0
             )
 
+    for op in sent:
+        op.wait_send()
+
+
+def correlate_kernel(n_src, total, lhs, rev, out_ref, rhs_a, rhs_b):
+    rows = out_ref.shape[1]
+    blocks = total // BLK + 4
+    scale = 1.0 / math.sqrt(total)
     width = BLK * (blocks + 1)
 
     def build(ref, pair):
@@ -249,41 +257,52 @@
     blocks = total // BLK + 4
     vmem = pl.BlockSpec(memory_space=pltpu.VMEM)
     dma = pltpu.SemaphoreType.DMA
-    everything = pl.pallas_call(
-        functools.partial(gather_kernel, n_tm, n_chan),
-        out_shape=jax.ShapeDtypeStruct((n_chan, n_tm, rows, t_dev), jnp.bfloat16),
+    padded_src = -(-n_src // 16) * 16
+    n_x = n_chan // 2
+    hbm = pl.BlockSpec(memory_space=pltpu.HBM)
+    lhs, rev = pl.pallas_call(
+        functools.partial(prepare_kernel, n_src, n_tm, n_chan),
+        out_shape=[
+            jax.ShapeDtypeStruct((4 * rows, BLK * blocks), jnp.bfloat16),
+            jax.ShapeDtypeStruct((padded_src, BLK * (blocks + 2)), jnp.float32),
+        ],
+        in_specs=[hbm] * 4,
+        out_specs=[vmem] * 2,
+        scratch_shapes=[
+            pltpu.VMEM((n_chan, n_tm, rows, t_dev), jnp.bfloat16),
+            pltpu.VMEM((rows, t_dev), jnp.bfloat16),
+            pltpu.VMEM((1, rows), jnp.int32),
+            pltpu.VMEM((1, fir_taps.shape[0]), jnp.float32),
+            pltpu.VMEM((1, panel_rows), jnp.int32),
+            pltpu.VMEM((8, 4 * BLK), jnp.float32),
+            pltpu.VMEM((rows + padded_src, total + 2 * PAD), jnp.bfloat16),
+            pltpu.VMEM((3, 2 * BLK, 4 * BLK), jnp.bfloat16),
+            pltpu.VMEM((3, 2 * BLK, 4 * BLK), jnp.bfloat16),
+            dma((4,)),
+            dma((n_tm,)),
+            dma((n_tm,)),
+            dma((n_x, n_tm)),
+            dma((n_x, n_tm)),
+            dma((n_x, n_tm)),
+            dma((n_x, n_tm)),
+        ],
+        compiler_params=pltpu.CompilerParams(
+            collective_id=0, has_side_effects=True, vmem_limit_bytes=40 * 2**20
+        ),
+        name="gather_and_filter",
+    )(record, quality.reshape(1, -1), fir_taps.reshape(1, -1), source_channels.reshape(1, -1))
+    return pl.pallas_call(
+        functools.partial(correlate_kernel, n_src, total),
+        out_shape=jax.ShapeDtypeStruct((n_src, rows, LAGS), jnp.float32),
         in_specs=[vmem] * 2,
         out_specs=vmem,
         scratch_shapes=[
-            dma((n_tm,)),
-            dma((n_tm,)),
-            dma((n_chan // 2, n_tm)),
-            dma((n_chan // 2, n_tm)),
-            dma((n_chan // 2, n_tm)),
-            dma((n_chan // 2, n_tm)),
-        ],
-        compiler_params=pltpu.CompilerParams(
-            collective_id=0, has_side_effects=True, vmem_limit_bytes=32 * 2**20
-        ),
-        name="gather_records",
-    )(record, quality.reshape(1, rows))
-    padded_src = -(-n_src // 16) * 16
-    return pl.pallas_call(
-        functools.partial(correlate_kernel, n_src),
-        out_shape=jax.ShapeDtypeStruct((n_src, rows, LAGS), jnp.float32),
-        in_specs=[vmem] * 3,
-        out_specs=vmem,
-        scratch_shapes=[
-            pltpu.VMEM((8, 4 * BLK), jnp.float32),
-            pltpu.VMEM((rows + padded_src, total + 2 * PAD), jnp.bfloat16),
-            pltpu.VMEM((padded_src, BLK * (blocks + 2)), jnp.float32),
-            pltpu.VMEM((4 * rows, BLK * blocks), jnp.bfloat16),
             pltpu.VMEM((BLK * blocks, 2 * BLK), jnp.bfloat16),
             pltpu.VMEM((BLK * blocks, 2 * BLK), jnp.bfloat16),
         ],
-        compiler_params=pltpu.CompilerParams(vmem_limit_bytes=56 * 2**20),
+        compiler_params=pltpu.CompilerParams(vmem_limit_bytes=40 * 2**20),
         name="correlate_all",
-    )(everything, fir_taps.reshape(1, -1), source_channels.reshape(1, -1))
+    )(lhs, rev)
 
 
 def solution(mesh):

time: 31.7 us -> 30.5 us (0.962)
  Pallas kernels: 29.2 us -> 27.5 us
  local copies, waits for them, and re-layouts: 2.2 us -> 2.75 us
    pallas_call x2, Pallas kernels: 29.2 us -> 27.5 us  [the longest x1 17 us: local(): pl.pallas_call(functools.partial(prepare_kernel, n_src, n_tm, n_chan), ou...]
    unnamed x6 -> x8, local copies, waits for them, and re-layouts: 2.2 us -> 2.75 us
where the time goes in v1:
time: 30.5 us; the launch traced here: 30.2 us
  Pallas kernels  27.5 us (90%)
  local copies, waits for them, and re-layouts  2.75 us (9%)
    pallas_call x1, Pallas kernels, local(): pl.pallas_call(functools.partial(prepare_kernel, n_src, n_tm, n_chan), ou...  17 us
    pallas_call x1, Pallas kernels, local(): pl.pallas_call(functools.partial(correlate_kernel, n_src, total), out_sha...  10.5 us
    unnamed x8, local copies, waits for them, and re-layouts  2.75 us

profile of v1, /device:TPU:1, one launch (start us, length us, event | category | flops | bytes accessed | tf_op | source)
XLA Modules:
  0.0 30.2 jit_solution(13350944365047556100)
XLA Ops:
  0.0 0.0 copy-start
  0.0 0.8 %copy-done = bf16[32,512]{1,0:T(8,128)(2,1)S(1)} copy-done((bf16[32,512]{1,0:T(8,128)(2,1)S(1)}, bf16[32,512]{1,0:T(8,128)(2,1)}, u32[]{:S(2)}) %copy-start) | copy-done | bytes 32792
  0.8 0.0 copy-start.1
  0.8 0.7 %copy-done.1 = f32[129]{0:T(256)S(1)} copy-done((f32[129]{0:T(256)S(1)}, f32[129]{0:T(256)}, u32[]{:S(2)}) %copy-start.1) | copy-done | bytes 540
  1.4 0.0 copy-start.2
  1.4 0.7 %copy-done.2 = s32[32]{0:T(128)S(1)} copy-done((s32[32]{0:T(128)S(1)}, s32[32]{0:T(128)}, u32[]{:S(2)}) %copy-start.2) | copy-done | bytes 152
  2.1 0.0 copy-start.3
  2.1 0.7 %copy-done.3 = s32[128]{0:T(128)S(1)} copy-done((s32[128]{0:T(128)S(1)}, s32[128]{0:T(128)}, u32[]{:S(2)}) %copy-start.3) | copy-done | bytes 536
  2.8 17.0 %gather_and_filter.1 = (bf16[128,2560]{1,0:T(8,128)(2,1)S(1)}, f32[32,2816]{1,0:T(8,128)S(1)}) custom-call(bf16[32,512]{1,0:T(8,128)(2,1)S(1)} %copy-done, s32[1,32]{1,0:T(1,128)S(1)} %bitcast.4, f32[1,129]{1,0:T(1,128)S(1)} %bitcast.3, s32[1,128]{1,0:T(1,128)S(1)} %bitcast.5), custom_call_target="tpu_custom_call" | custom-call | tf_op jit(solution)/shard_map/gather_and_filter/pallas_call | solution.py:263
  19.7 10.5 %correlate_all.1 = f32[32,32,512]{2,1,0:T(8,128)} custom-call(bf16[128,2560]{1,0:T(8,128)(2,1)S(1)} %get-tuple-element.7.lhs, f32[32,2816]{1,0:T(8,128)S(1)} %get-tuple-element.8.rev), custom_call_target="tpu_custom_call" | custom-call | tf_op jit(solution)/shard_map/correlate_all/pallas_call | solution.py:294
Async XLA Ops:
  0.0 0.8 %copy-start = (bf16[32,512]{1,0:T(8,128)(2,1)S(1)}, bf16[32,512]{1,0:T(8,128)(2,1)}, u32[]{:S(2)}) copy-start(bf16[32,512]{1,0:T(8,128)(2,1)} %rec_hbm.1) | copy-start | bytes 98308
  0.8 0.7 %copy-start.1 = (f32[129]{0:T(256)S(1)}, f32[129]{0:T(256)}, u32[]{:S(2)}) copy-start(f32[129]{0:T(256)} %param.6) | copy-start | bytes 1552
  1.4 0.7 %copy-start.2 = (s32[32]{0:T(128)S(1)}, s32[32]{0:T(128)}, u32[]{:S(2)}) copy-start(s32[32]{0:T(128)} %param.5) | copy-start | bytes 388
  2.1 0.7 %copy-start.3 = (s32[128]{0:T(128)S(1)}, s32[128]{0:T(128)}, u32[]{:S(2)}) copy-start(s32[128]{0:T(128)} %param.7) | copy-start | bytes 1540

commit v2 on v1

--- a/solution.py
+++ b/solution.py
@@ -287,7 +287,7 @@
             dma((n_x, n_tm)),
         ],
         compiler_params=pltpu.CompilerParams(
-            collective_id=0, has_side_effects=True, vmem_limit_bytes=40 * 2**20
+            collective_id=0, has_side_effects=True, vmem_limit_bytes=62 * 2**20 + 800 * 2**10
         ),
         name="gather_and_filter",
     )(record, quality.reshape(1, -1), fir_taps.reshape(1, -1), source_channels.reshape(1, -1))
@@ -300,7 +300,7 @@
             pltpu.VMEM((BLK * blocks, 2 * BLK), jnp.bfloat16),
             pltpu.VMEM((BLK * blocks, 2 * BLK), jnp.bfloat16),
         ],
-        compiler_params=pltpu.CompilerParams(vmem_limit_bytes=40 * 2**20),
+        compiler_params=pltpu.CompilerParams(vmem_limit_bytes=62 * 2**20 + 800 * 2**10),
         name="correlate_all",
     )(lhs, rev)
 

time: 30.5 us -> 29.8 us (0.977)
  local copies, waits for them, and re-layouts: 2.75 us -> 0 us
  Pallas kernels: 27.5 us -> 29.6 us
    unnamed x8 -> x0, local copies, waits for them, and re-layouts: 2.75 us -> none
    pallas_call x1, Pallas kernels: 10.5 us -> 11.7 us  [local(): pl.pallas_call(functools.partial(correlate_kernel, n_src, total), out_sha...]
    pallas_call x1, Pallas kernels: 17 us -> 17.9 us  [local(): pl.pallas_call(functools.partial(prepare_kernel, n_src, n_tm, n_chan), ou...]
where the time goes in v2:
time: 29.8 us; the launch traced here: 29.6 us
  Pallas kernels  29.6 us (99%)
    pallas_call x1, Pallas kernels, local(): pl.pallas_call(functools.partial(prepare_kernel, n_src, n_tm, n_chan), ou...  17.9 us
    pallas_call x1, Pallas kernels, local(): pl.pallas_call(functools.partial(correlate_kernel, n_src, total), out_sha...  11.7 us

profile of v2, /device:TPU:1, one launch (start us, length us, event | category | flops | bytes accessed | tf_op | source)
XLA Modules:
  0.0 29.6 jit_solution(15911906175772280522)
XLA Ops:
  0.0 17.9 %gather_and_filter.1 = (bf16[128,2560]{1,0:T(8,128)(2,1)}, f32[32,2816]{1,0:T(8,128)}) custom-call(bf16[32,512]{1,0:T(8,128)(2,1)} %rec_hbm.1, s32[1,32]{1,0:T(1,128)} %bitcast.4, f32[1,129]{1,0:T(1,128)} %bitcast.3, s32[1,128]{1,0:T(1,128)} %bitcast.5), custom_call_target="tpu_custom_call" | custom-call | tf_op jit(solution)/shard_map/gather_and_filter/pallas_call | solution.py:263
  17.9 11.7 %correlate_all.1 = f32[32,32,512]{2,1,0:T(8,128)} custom-call(bf16[128,2560]{1,0:T(8,128)(2,1)} %get-tuple-element.7.lhs, f32[32,2816]{1,0:T(8,128)} %get-tuple-element.8.rev), custom_call_target="tpu_custom_call" | custom-call | tf_op jit(solution)/shard_map/correlate_all/pallas_call | solution.py:294
